TPU v7x, 32 devices: a whole 2x2x4 slice. The times are simulated.
32 devices in a mesh: mp: 2 (over y), dp: 4 (over x, core), seq: 4 (over z).
Axes of the slice: x: 2, y: 2, z: 4, core: 2. Of those that a mesh axis runs over, the one named last changes fastest.
Arguments:
- tokens: bfloat16 [32, 1024, 1024], P('dp', 'seq'), may hold values from -6 to 6
- cotangent: bfloat16 [32, 1024, 1024], P('dp', 'seq'), may hold values from -6 to 6
- lengths: int32 [32], P('dp'), may hold values from 256 to 1024, as said below
- orientation: int32 [32], P('dp'), may hold values from 0 to 1
- joint_weight: float32 [1024, 3072], P(('dp', 'seq'), 'mp'), may hold values from -0.1875 to 0.1875
- output_weight: float32 [1024, 1024], P('mp', ('dp', 'seq')), may hold values from -1 to 1
- expand_weight: float32 [1024, 4096], P(('dp', 'seq'), 'mp'), may hold values from -0.1875 to 0.1875
- shrink_weight: float32 [4096, 1024], P('mp', ('dp', 'seq')), may hold values from -0.09375 to 0.09375
- norm_params: float32 [3, 1024], P(None, 'mp')
- expand_bias: float32 [4096], P('mp'), may hold values from -2 to 2
- norm_moment: float32 [3, 1024], P(None, 'mp'), may hold values from 3276 to 13107
- bias_moment: float32 [4096], P('mp'), may hold values from 204 to 819
- joint_left: float32 [1024, 128], P(('dp', 'seq'), 'mp')
- joint_right: float32 [24576, 3072], P(('dp', 'seq'), 'mp')
- joint_left_root: float32 [1024, 128], P(('dp', 'seq'), 'mp')
- joint_right_root: float32 [24576, 3072], P(('dp', 'seq'), 'mp')
- output_left: float32 [8192, 1024], P(('dp', 'seq'), 'mp')
- output_right: float32 [1024, 128], P(('dp', 'seq'), 'mp')
- output_left_root: float32 [8192, 1024], P(('dp', 'seq'), 'mp')
- output_right_root: float32 [1024, 128], P(('dp', 'seq'), 'mp')
- expand_left: float32 [1024, 128], P(('dp', 'seq'), 'mp')
- expand_right: float32 [32768, 4096], P(('dp', 'seq'), 'mp')
- expand_left_root: float32 [1024, 128], P(('dp', 'seq'), 'mp')
- expand_right_root: float32 [32768, 4096], P(('dp', 'seq'), 'mp')
- shrink_left: float32 [32768, 4096], P(('dp', 'seq'), 'mp')
- shrink_right: float32 [1024, 128], P(('dp', 'seq'), 'mp')
- shrink_left_root: float32 [32768, 4096], P(('dp', 'seq'), 'mp')
- shrink_right_root: float32 [1024, 128], P(('dp', 'seq'), 'mp')
Outputs:
- block_output: bfloat16 [32, 1024, 1024], P('dp', 'seq', 'mp')
- input_grad: float32 [32, 1024, 1024], P('dp', 'seq')
- joint_grad: float32 [1024, 3072], P(('dp', 'seq'), 'mp')
- output_grad: float32 [1024, 1024], P('mp', ('dp', 'seq'))
- expand_grad: float32 [1024, 4096], P(('dp', 'seq'), 'mp')
- shrink_grad: float32 [4096, 1024], P('mp', ('dp', 'seq'))
- norm_grad: float32 [3, 1024], P(None, 'mp')
- bias_grad: float32 [4096], P('mp')
- joint_left_new: float32 [1024, 128], P(('dp', 'seq'), 'mp')
- joint_right_new: float32 [24576, 3072], P(('dp', 'seq'), 'mp')
- output_left_new: float32 [8192, 1024], P(('dp', 'seq'), 'mp')
- output_right_new: float32 [1024, 128], P(('dp', 'seq'), 'mp')
- expand_left_new: float32 [1024, 128], P(('dp', 'seq'), 'mp')
- expand_right_new: float32 [32768, 4096], P(('dp', 'seq'), 'mp')
- shrink_left_new: float32 [32768, 4096], P(('dp', 'seq'), 'mp')
- shrink_right_new: float32 [1024, 128], P(('dp', 'seq'), 'mp')
- joint_weight_new: float32 [1024, 3072], P(('dp', 'seq'), 'mp')
- output_weight_new: float32 [1024, 1024], P('mp', ('dp', 'seq'))
- expand_weight_new: float32 [1024, 4096], P(('dp', 'seq'), 'mp')
- shrink_weight_new: float32 [4096, 1024], P('mp', ('dp', 'seq'))
- norm_moment_new: float32 [3, 1024], P(None, 'mp')
- bias_moment_new: float32 [4096], P('mp')
- norm_params_new: float32 [3, 1024], P(None, 'mp')
- bias_new: float32 [4096], P('mp')
Inputs may be any that keep to these rules, and one draw needn't show every extreme that they name: `lengths`: sequences 0 to 7, 8 to 15 and so on each hold at least one of length 1024. `orientation`: 1 marks a reversed protein, whose padding stands before position 1024 - lengths; 0 a forward one, padded after lengths - 1.
All inputs are finite; a program needn't handle non-finite values.
Results may differ from a plain program's by a relative error of at most 0.005.
The roundings to bfloat16 on the way count: a program that leaves them out, or rounds other values in their place, can miss the bound.
Values may be sent and summed in bfloat16 or wider, within the bound.
No kernel may reach another device: no remote copies, remote signals or barrier semaphores. Data moves between devices by JAX's collectives and lax.ppermute only.
A program may use at most 512 MiB of HBM per device.

v0:
```python
import math

import jax
import jax.numpy as jnp
from jax import lax
from jax.sharding import PartitionSpec as P

D = 1024
HS = 64
ROT = 32
FF = 4096
LEN = 1024


highest = lax.Precision.HIGHEST
norm_eps = 1e-05
beta_stats = 0.95
beta_moment = 0.95
rate_matrix = 0.5
rate_vector = 0.03


def rotate(values, positions):
    half_rot = ROT // 2
    frequency = 10000.0 ** (-2.0 * jnp.arange(half_rot, dtype=jnp.float32) / ROT)
    angles = positions[:, None] * frequency[None, :]
    cosine = jnp.cos(angles)[:, None, :]
    sine_part = jnp.sin(angles)[:, None, :]
    paired = values[..., :ROT].reshape(values.shape[:-1] + (half_rot, 2))
    even_part = paired[..., 0]
    odd_part = paired[..., 1]
    turned = jnp.stack(
        [even_part * cosine - odd_part * sine_part, odd_part * cosine + even_part * sine_part],
        axis=-1,
    )
    return jnp.concatenate([turned.reshape(values.shape[:-1] + (ROT,)), values[..., ROT:]], axis=-1)


def allowed_keys(query_pos, key_pos, lengths, orientation):
    valid = jnp.where(
        orientation[:, None] == 0,
        key_pos[None, :] < lengths[:, None],
        key_pos[None, :] >= LEN - lengths[:, None],
    )
    causal = key_pos[None, :] <= query_pos[:, None]
    itself = key_pos[None, :] == query_pos[:, None]
    return causal[None] & (valid[:, None, :] | itself[None])


def normed_rows(inputs, gain, shift):
    centred = inputs - jnp.mean(inputs, -1, keepdims=True)
    spread = jnp.mean(centred * centred, -1, keepdims=True)
    return centred * lax.rsqrt(spread + norm_eps) * gain + shift


def gelu_tanh(values):
    return jax.nn.gelu(values, approximate=True)


def contract_rows(left_side, right_side):
    return lax.dot_general(
        left_side, right_side, (((0,), (0,)), ((), ())), preferred_element_type=jnp.float32
    )


def contract_cols(left_side, right_side):
    return lax.dot_general(
        left_side, right_side, (((1,), (1,)), ((), ())), preferred_element_type=jnp.float32
    )


def shampoo(gradient, weight, left, right, left_root, right_root, fan):
    left_new = beta_stats * left + (1.0 - beta_stats) * jnp.dot(
        gradient, gradient.T, precision=highest
    )
    right_new = beta_stats * right + (1.0 - beta_stats) * jnp.dot(
        gradient.T, gradient, precision=highest
    )
    turned = jnp.dot(jnp.dot(left_root, gradient, precision=highest), right_root, precision=highest)
    square = jnp.mean(turned * turned)
    return (
        left_new,
        right_new,
        weight - rate_matrix / math.sqrt(fan) * turned * lax.rsqrt(square + 1e-06),
    )


def diagonal_rule(params, moment, gradient):
    moment_new = beta_moment * moment + (1.0 - beta_moment) * gradient * gradient
    return (moment_new, params - rate_vector * gradient / (jnp.sqrt(moment_new) + 1e-08))


def body(
    tokens,
    cotangent,
    lengths,
    orientation,
    joint_weight,
    output_weight,
    expand_weight,
    shrink_weight,
    norm_params,
    expand_bias,
    norm_moment,
    bias_moment,
    joint_left,
    joint_right,
    joint_left_root,
    joint_right_root,
    output_left,
    output_right,
    output_left_root,
    output_right_root,
    expand_left,
    expand_right,
    expand_left_root,
    expand_right_root,
    shrink_left,
    shrink_right,
    shrink_left_root,
    shrink_right_root,
):
    joint_full, expand_full = (
        lax.all_gather(joint_weight.astype(jnp.bfloat16), ("dp", "seq"), axis=0, tiled=True),
        lax.all_gather(expand_weight.astype(jnp.bfloat16), ("dp", "seq"), axis=0, tiled=True),
    )
    output_full, shrink_full = (
        lax.all_gather(output_weight.astype(jnp.bfloat16), ("dp", "seq"), axis=1, tiled=True),
        lax.all_gather(shrink_weight.astype(jnp.bfloat16), ("dp", "seq"), axis=1, tiled=True),
    )
    vectors = lax.all_gather(norm_params, "mp", axis=1, tiled=True)
    seqs_here, local_len, width = tokens.shape
    row_count = seqs_here * local_len
    heads_here = joint_full.shape[1] // (3 * HS)
    shard_width = norm_params.shape[1]
    mp_index = lax.axis_index("mp")
    seq_index = lax.axis_index("seq")
    score_scale = 1.0 / math.sqrt(HS)

    def own_share(values):
        return lax.dynamic_slice_in_dim(
            values, mp_index * shard_width, shard_width, values.ndim - 1
        )

    inputs32 = tokens.astype(jnp.float32)
    normed_low = (
        normed_rows(inputs32, vectors[0], vectors[1]).astype(jnp.bfloat16).reshape(row_count, width)
    )
    joint_cols = jnp.dot(normed_low, joint_full, preferred_element_type=jnp.float32)
    joint_cols = joint_cols.reshape(seqs_here, local_len, 3, heads_here, HS)
    query_ids = seq_index * local_len + jnp.arange(local_len, dtype=jnp.int32)
    key_ids = jnp.arange(LEN, dtype=jnp.int32)
    positions = query_ids.astype(jnp.float32)

    def turn_pair(query_part, key_part):
        return (rotate(query_part, positions), rotate(key_part, positions))

    (query_rot, key_rot), turn_back = jax.vjp(turn_pair, joint_cols[:, :, 0], joint_cols[:, :, 1])
    query_low = query_rot.astype(jnp.bfloat16)
    key_low = key_rot.astype(jnp.bfloat16)
    value_low = joint_cols[:, :, 2].astype(jnp.bfloat16)
    cot_low = cotangent.reshape(row_count, width)
    back_context = contract_cols(cot_low, output_full).astype(jnp.bfloat16)
    back_context = back_context.reshape(seqs_here, local_len, heads_here, HS)
    allowed = allowed_keys(query_ids, key_ids, lengths, orientation)[:, None]

    def masked_scores(key_set):
        scores = (
            jnp.einsum("sqhd,skhd->shqk", query_low, key_set, preferred_element_type=jnp.float32)
            * score_scale
        )
        return jnp.where(allowed, scores, -1e30)

    key_all, value_all = (
        lax.all_gather(key_low, "seq", axis=1, tiled=True),
        lax.all_gather(value_low, "seq", axis=1, tiled=True),
    )
    masked = masked_scores(key_all)
    row_top = jnp.max(masked, -1, keepdims=True)
    exponent = jnp.where(allowed, jnp.exp(masked - row_top), 0.0)
    row_total = jnp.sum(exponent, -1, keepdims=True)
    attend = exponent / row_total
    log_total = row_top + jnp.log(row_total)
    attend_low = attend.astype(jnp.bfloat16)
    context = jnp.einsum(
        "shqk,skhd->sqhd", attend_low, value_all, preferred_element_type=jnp.float32
    )
    context_low = context.astype(jnp.bfloat16).reshape(row_count, heads_here * HS)
    key_again, value_again = (
        lax.all_gather(key_low, "seq", axis=1, tiled=True),
        lax.all_gather(value_low, "seq", axis=1, tiled=True),
    )
    attend_again = jnp.where(allowed, jnp.exp(masked_scores(key_again) - log_total), 0.0)
    back_attend = jnp.einsum(
        "sqhd,skhd->shqk", back_context, value_again, preferred_element_type=jnp.float32
    )
    row_delta = jnp.sum(attend_again * back_attend, -1, keepdims=True)
    grad_scores = (attend_again * (back_attend - row_delta)).astype(jnp.bfloat16)
    grad_query = (
        jnp.einsum("shqk,skhd->sqhd", grad_scores, key_again, preferred_element_type=jnp.float32)
        * score_scale
    )
    grad_key = (
        jnp.einsum("shqk,sqhd->skhd", grad_scores, query_low, preferred_element_type=jnp.float32)
        * score_scale
    )
    grad_value = jnp.einsum(
        "shqk,sqhd->skhd",
        attend_again.astype(jnp.bfloat16),
        back_context,
        preferred_element_type=jnp.float32,
    )
    key_part, value_part = (
        lax.psum_scatter(grad_key, "seq", scatter_dimension=1, tiled=True),
        lax.psum_scatter(grad_value, "seq", scatter_dimension=1, tiled=True),
    )
    query_back, key_back = turn_back((grad_query, key_part))
    grad_joint = jnp.stack([query_back, key_back, value_part], axis=2).reshape(
        row_count, 3 * heads_here * HS
    )
    grad_joint = grad_joint.astype(jnp.bfloat16)
    pre_act = jnp.dot(normed_low, expand_full, preferred_element_type=jnp.float32) + expand_bias
    active, gelu_back = jax.vjp(gelu_tanh, pre_act)
    active_low = active.astype(jnp.bfloat16)
    branch = jnp.dot(context_low, output_full, preferred_element_type=jnp.float32)
    branch = branch + jnp.dot(active_low, shrink_full, preferred_element_type=jnp.float32)
    summed = lax.psum_scatter(
        branch.reshape(seqs_here, local_len, width), "mp", scatter_dimension=2, tiled=True
    )
    block_output = (own_share(inputs32) + summed + norm_params[2]).astype(jnp.bfloat16)
    back_active = contract_cols(cot_low, shrink_full)
    grad_pre = gelu_back(back_active)[0].astype(jnp.bfloat16)
    input_part = contract_cols(grad_joint, joint_full) + contract_cols(grad_pre, expand_full)
    input_part = input_part.reshape(seqs_here, local_len, width)
    cot32 = cotangent.astype(jnp.float32)
    back_normed = lax.psum(input_part, "mp")
    unused_out, norm_back = jax.vjp(normed_rows, inputs32, vectors[0], vectors[1])
    grad_inputs, grad_gain, grad_shift = norm_back(back_normed)
    input_grad = cot32 + grad_inputs
    gain_term = own_share(grad_gain)
    shift_term = own_share(grad_shift)
    out_bias_term = own_share(jnp.sum(cot32, (0, 1)))
    bias_term = jnp.sum(grad_pre.astype(jnp.float32), 0)
    joint_term = contract_rows(normed_low, grad_joint)
    expand_term = contract_rows(normed_low, grad_pre)
    output_term = contract_rows(context_low, cot_low)
    shrink_term = contract_rows(active_low, cot_low)
    joint_grad, expand_grad = (
        lax.psum_scatter(joint_term, ("dp", "seq"), scatter_dimension=0, tiled=True),
        lax.psum_scatter(expand_term, ("dp", "seq"), scatter_dimension=0, tiled=True),
    )
    output_grad, shrink_grad = (
        lax.psum_scatter(output_term, ("dp", "seq"), scatter_dimension=1, tiled=True),
        lax.psum_scatter(shrink_term, ("dp", "seq"), scatter_dimension=1, tiled=True),
    )
    vector_terms = jnp.stack([gain_term, shift_term, out_bias_term])
    norm_grad, bias_grad = lax.psum((vector_terms, bias_term), ("dp", "seq"))
    joint_left_new, joint_right_new, joint_weight_new = shampoo(
        joint_grad, joint_weight, joint_left, joint_right, joint_left_root, joint_right_root, D
    )
    output_left_new, output_right_new, output_weight_new = shampoo(
        output_grad,
        output_weight,
        output_left,
        output_right,
        output_left_root,
        output_right_root,
        D // 32,
    )
    expand_left_new, expand_right_new, expand_weight_new = shampoo(
        expand_grad,
        expand_weight,
        expand_left,
        expand_right,
        expand_left_root,
        expand_right_root,
        D,
    )
    shrink_left_new, shrink_right_new, shrink_weight_new = shampoo(
        shrink_grad,
        shrink_weight,
        shrink_left,
        shrink_right,
        shrink_left_root,
        shrink_right_root,
        FF,
    )
    norm_moment_new, norm_params_new = diagonal_rule(norm_params, norm_moment, norm_grad)
    bias_moment_new, bias_new = diagonal_rule(expand_bias, bias_moment, bias_grad)
    return (
        block_output,
        input_grad,
        joint_grad,
        output_grad,
        expand_grad,
        shrink_grad,
        norm_grad,
        bias_grad,
        joint_left_new,
        joint_right_new,
        output_left_new,
        output_right_new,
        expand_left_new,
        expand_right_new,
        shrink_left_new,
        shrink_right_new,
        joint_weight_new,
        output_weight_new,
        expand_weight_new,
        shrink_weight_new,
        norm_moment_new,
        bias_moment_new,
        norm_params_new,
        bias_new,
    )


def solution(mesh):
    placed = (
        P("dp", "seq", None),
        P("dp", "seq", None),
        P("dp"),
        P("dp"),
        P(("dp", "seq"), "mp"),
        P("mp", ("dp", "seq")),
        P(("dp", "seq"), "mp"),
        P("mp", ("dp", "seq")),
        P(None, "mp"),
        P("mp"),
        P(None, "mp"),
        P("mp"),
        P(("dp", "seq"), "mp"),
        P(("dp", "seq"), "mp"),
        P(("dp", "seq"), "mp"),
        P(("dp", "seq"), "mp"),
        P(("dp", "seq"), "mp"),
        P(("dp", "seq"), "mp"),
        P(("dp", "seq"), "mp"),
        P(("dp", "seq"), "mp"),
        P(("dp", "seq"), "mp"),
        P(("dp", "seq"), "mp"),
        P(("dp", "seq"), "mp"),
        P(("dp", "seq"), "mp"),
        P(("dp", "seq"), "mp"),
        P(("dp", "seq"), "mp"),
        P(("dp", "seq"), "mp"),
        P(("dp", "seq"), "mp"),
    )
    return jax.shard_map(
        body,
        mesh=mesh,
        in_specs=placed,
        out_specs=(
            P("dp", "seq", "mp"),
            P("dp", "seq", None),
            P(("dp", "seq"), "mp"),
            P("mp", ("dp", "seq")),
            P(("dp", "seq"), "mp"),
            P("mp", ("dp", "seq")),
            P(None, "mp"),
            P("mp"),
            P(("dp", "seq"), "mp"),
            P(("dp", "seq"), "mp"),
            P(("dp", "seq"), "mp"),
            P(("dp", "seq"), "mp"),
            P(("dp", "seq"), "mp"),
            P(("dp", "seq"), "mp"),
            P(("dp", "seq"), "mp"),
            P(("dp", "seq"), "mp"),
            P(("dp", "seq"), "mp"),
            P("mp", ("dp", "seq")),
            P(("dp", "seq"), "mp"),
            P("mp", ("dp", "seq")),
            P(None, "mp"),
            P("mp"),
            P(None, "mp"),
            P("mp"),
        ),
        check_vma=False,
    )
```

profile of v0, /device:TPU:0, one launch (start us, length us, event | category | flops | bytes accessed | tf_op | source)
XLA Modules:
  0.0 1898.9 jit_solution(16374606328207381390)
XLA Ops:
  24.9 34.1 %all-gather.8.cloned.1.call-done = bf16[1024,1536]{1,0:T(8,128)(2,1)} async-done(((bf16[64,1536]{1,0:T(8,128)(2,1)}), bf16[1024,1536]{1,0:T(8,128)(2,1)}) %all-gather.8.cloned.1.call-update) | async-done | bytes 3145744 | tf_op jit(solution)/shard_map/all_gather | solution.py:124
  118.9 132.5 %all-gather.10.cloned.1.call-done = bf16[8,1024,8,64]{1,3,2,0:T(8,128)(2,1)} async-done(((bf16[8,256,8,64]{1,3,2,0:T(8,128)(2,1)}), bf16[8,1024,8,64]{1,3,2,0:T(8,128)(2,1)}) %all-gather.10.cloned.1.call-update) | async-done | bytes 8388624 | tf_op jit(solution)/shard_map/all_gather | solution.py:175
  251.3 30.8 %fusion.1 = (f32[8,8,256]{2,1,0:T(8,128)S(1)}, f32[8,8,256,1024]{3,2,1,0:T(8,128)}) fusion(pred[8,256,1024]{2,1,0:T(8,128)(4,1)S(1)} %or_and_fusion, bf16[8,1024,8,64]{1,3,2,0:T(8,128)(2,1)} %all-gather.10.cloned.1.call-done, bf16[8,256,8,32]{1,3,2,0:T(8,128)(2,1)} %slice.88, bf16[8,256,8,32]{1,3,2,0:T(8,128)(2,1)} %reshape.311), kind=kOutput, calls=%fused_computation.7 | convolution fusion | flops 2201993216 | bytes 79757312 | tf_op jit(solution)/shard_map/sqhd,skhd->shqk/dot_general | solution.py:169
  282.1 22.4 %fusion = f32[8,8,256]{2,1,0:T(8,128)S(1)} fusion(f32[8,8,256,1024]{3,2,1,0:T(8,128)} %get-tuple-element.65, f32[8,8,256]{2,1,0:T(8,128)S(1)} %get-tuple-element.64, pred[8,256,1024]{2,1,0:T(8,128)(4,1)S(1)} %or_and_fusion), kind=kLoop, calls=%fused_computation.6 | loop fusion | flops 83869696 | bytes 69337088 | tf_op jit(solution)/shard_map/reduce_sum | solution.py:181
  304.5 96.3 %all-gather.18.cloned.1.call-done = bf16[8,1024,1,8,64]{1,4,3,2,0:T(8,128)(2,1)} async-done(((bf16[8,256,1,8,64]{1,4,3,2,0:T(8,128)(2,1)}), bf16[8,1024,1,8,64]{1,4,3,2,0:T(8,128)(2,1)}) %all-gather.18.cloned.1.call-update) | async-done | bytes 8388624 | tf_op jit(solution)/shard_map/all_gather | solution.py:176
  400.8 29.8 %convert_bitcast_fusion = bf16[8,256,8,64]{1,3,2,0:T(8,128)(2,1)S(1)} fusion(f32[8,8,256,1024]{3,2,1,0:T(8,128)} %get-tuple-element.65, f32[8,8,256]{2,1,0:T(8,128)S(1)} %fusion, f32[8,8,256]{2,1,0:T(8,128)S(1)} %get-tuple-element.64, pred[8,256,1024]{2,1,0:T(8,128)(4,1)S(1)} %or_and_fusion, bf16[8,1024,1,8,64]{1,4,3,2,0:T(8,128)(2,1)} %all-gather.18.cloned.1.call-done), kind=kOutput, calls=%fused_computation.60 | convolution fusion | flops 2249195520 | bytes 79822848 | tf_op jit(solution)/shard_map/shqk,skhd->sqhd/dot_general | solution.py:185
  437.8 59.9 %reduce-scatter.16.cloned.1.call-done = f32[512,64]{0,1:T(8,128)} async-done(((f32[512,1024]{0,1:T(8,128)}), f32[512,64]{0,1:T(8,128)}) %reduce-scatter.16.cloned.1.call-update) | async-done | bytes 131088 | tf_op jit(solution)/shard_map/reduce_scatter | solution.py:253
  505.8 33.4 %all-gather.12.cloned.1.call-done = bf16[512,1024]{0,1:T(8,128)(2,1)} async-done(((bf16[512,64]{0,1:T(8,128)(2,1)}), bf16[512,1024]{0,1:T(8,128)(2,1)}) %all-gather.12.cloned.1.call-update) | async-done | bytes 1048592 | tf_op jit(solution)/shard_map/all_gather | solution.py:128
  556.8 55.4 %multiply_reduce_fusion = (f32[8,8,256]{2,1,0:T(8,128)S(1)}, f32[8,8,256,1024]{3,2,1,0:T(8,128)}) fusion(f32[8,8,256]{2,1,0:T(8,128)S(1)} %log_add_fusion, f32[8,8,256,1024]{3,2,1,0:T(8,128)} %get-tuple-element.65, pred[8,256,1024]{2,1,0:T(8,128)(4,1)S(1)} %or_and_fusion, bf16[8,256,8,64]{1,3,2,0:T(8,128)(2,1)} %copy.58, ...), kind=kOutput, calls=%fused_computation.1 | convolution fusion | flops 2248130560 | bytes 146931712 | tf_op jit(solution)/shard_map/sqhd,skhd->shqk/dot_general | solution.py:194
  612.1 54.3 %multiply_convert_fusion = bf16[8,8,256,1024]{3,2,1,0:T(8,128)(2,1)} fusion(f32[8,8,256,1024]{3,2,1,0:T(8,128)} %get-tuple-element.69, f32[8,8,256]{2,1,0:T(8,128)S(1)} %get-tuple-element.68, f32[8,8,256]{2,1,0:T(8,128)S(1)} %log_add_fusion, f32[8,8,256,1024]{3,2,1,0:T(8,128)} %get-tuple-element.65, pred[8,256,1024]{2,1,0:T(8,128)(4,1)S(1)} %or_and_fusion), kind=kLoop, calls=%fused_computation | loop fusion | flops 117440512 | bytes 170000384 | tf_op jit(solution)/shard_map/convert_element_type | solution.py:198
  666.4 22.7 %multiply_bitcast_fusion = f32[8,1024,8,64]{1,3,2,0:T(8,128)} fusion(bf16[8,8,256,1024]{3,2,1,0:T(8,128)(2,1)} %multiply_convert_fusion, bf16[8,256,8,32]{1,3,2,0:T(8,128)(2,1)S(1)} %copy-done.11, bf16[8,256,8,32]{1,3,2,0:T(8,128)(2,1)} %reshape.311), kind=kOutput, calls=%fused_computation.23 | convolution fusion | flops 2155872256 | bytes 52428800 | tf_op jit(solution)/shard_map/shqk,sqhd->skhd/dot_general | solution.py:204
  689.1 32.5 %fusion.13 = f32[8,1024,8,64]{1,3,2,0:T(8,128)} fusion(bf16[8,256,8,64]{1,3,2,0:T(8,128)(2,1)} %copy.58, f32[8,8,256]{2,1,0:T(8,128)S(1)} %log_add_fusion, f32[8,8,256,1024]{3,2,1,0:T(8,128)} %get-tuple-element.65, pred[8,256,1024]{2,1,0:T(8,128)(4,1)S(1)} %or_and_fusion), kind=kOutput, calls=%fused_computation.31 | convolution fusion | flops 2231369728 | bytes 88145920 | tf_op jit(solution)/shard_map/shqk,sqhd->skhd/dot_general | solution.py:207
  737.1 26.7 %convert_reduce_fusion = (f32[2048]{0:T(1024)}, bf16[2048,2048]{1,0:T(8,128)(2,1)S(1)}, bf16[2048,2048]{1,0:T(8,128)(2,1)}) fusion(f32[2048,2048]{1,0:T(8,128)} %fusion.49, f32[2048]{0:T(1024)S(1)} %copy-done.48, bf16[2048,1024]{1,0:T(8,128)(2,1)} %bitcast.155, bf16[2048,1024]{0,1:T(8,128)(2,1)} %all-gather.16.cloned.1.call-done), kind=kOutput, calls=%fused_computation.22 | convolution fusion | flops 8694790144 | bytes 41959424 | tf_op jit(solution)/shard_map/dot_general | solution.py:67
  827.7 18.4 multiply_bitcast_fusion.1
  851.0 117.6 %reduce-scatter.10.cloned.1.call-done = f32[8,256,8,64]{1,3,2,0:T(8,128)} async-done(((f32[8,1024,8,64]{1,3,2,0:T(8,128)}), f32[8,256,8,64]{1,3,2,0:T(8,128)}) %reduce-scatter.10.cloned.1.call-update) | async-done | bytes 4194320 | tf_op jit(solution)/shard_map/reduce_scatter | solution.py:214
  1000.7 252.0 %reduce-scatter.12.cloned.1.call-done = f32[8,256,8,64]{1,3,2,0:T(8,128)} async-done(((f32[8,1024,8,64]{1,3,2,0:T(8,128)}), f32[8,256,8,64]{1,3,2,0:T(8,128)}) %reduce-scatter.12.cloned.1.call-update) | async-done | bytes 4194320 | tf_op jit(solution)/shard_map/reduce_scatter | solution.py:215
  1284.9 78.1 %reduce-scatter.18.cloned.1.call-done = f32[64,2048]{1,0:T(8,128)} async-done(((f32[1024,2048]{1,0:T(8,128)}), f32[64,2048]{1,0:T(8,128)}) %reduce-scatter.18.cloned.1.call-update) | async-done | bytes 524304 | tf_op jit(solution)/shard_map/reduce_scatter | solution.py:250
  1394.7 78.0 %reduce-scatter.20.cloned.1.call-done = f32[2048,64]{0,1:T(8,128)} async-done(((f32[2048,1024]{0,1:T(8,128)}), f32[2048,64]{0,1:T(8,128)}) %reduce-scatter.20.cloned.1.call-update) | async-done | bytes 524304 | tf_op jit(solution)/shard_map/reduce_scatter | solution.py:254
  1472.6 21.9 %fusion.59 = f32[64,2048]{1,0:T(8,128)S(1)} fusion(f32[2048,64]{0,1:T(8,128)} %reduce-scatter.20.cloned.1.call-done, f32[2048,2048]{1,0:T(8,128)} %param.54), kind=kOutput, calls=%fused_computation.136 | convolution fusion | flops 3221225472 | bytes 17825792 | tf_op jit(solution)/shard_map/dot_general | solution.py:79
  1501.7 19.7 %multiply_add_fusion.1 = f32[2048,2048]{1,0:T(8,128)} fusion(f32[2048,2048]{1,0:T(8,128)} %param.49, f32[64,2048]{1,0:T(8,128)S(1)} %copy-done.7), kind=kOutput, calls=%fused_computation.21 | convolution fusion | flops 3233808384 | bytes 34078720 | tf_op jit(solution)/shard_map/dot_general | solution.py:76
  1521.5 17.9 multiply_add_fusion
  1542.3 32.2 %reduce-scatter.8.cloned.1.call-done = f32[8,256,512]{2,1,0:T(8,128)} async-done(((f32[8,256,1024]{2,1,0:T(8,128)}), f32[8,256,512]{2,1,0:T(8,128)}) %reduce-scatter.8.cloned.1.call-update) | async-done | bytes 4194320 | tf_op jit(solution)/shard_map/reduce_scatter | solution.py:227
  1580.4 194.6 %all-reduce.11.cloned.1.call-done = f32[8,256,1024]{2,1,0:T(8,128)} async-done(((f32[8,256,1024]{2,1,0:T(8,128)}), f32[8,256,1024]{2,1,0:T(8,128)}) %all-reduce.11.cloned.1.call-update) | async-done | bytes 8388624 | tf_op jit(solution)/shard_map/psum | solution.py:236
  1793.7 63.5 %all-reduce.8 = (f32[3,512]{1,0:T(4,128)S(1)}, f32[2048]{0:T(1024)S(1)}) all-reduce(f32[3,512]{1,0:T(4,128)S(1)} %pad_maximum_fusion.6, f32[2048]{0:T(1024)S(1)} %copy-done.54), channel_id=1, replica_groups=mesh['mp'=2,'dp'=4,'seq'=4] {'dp','seq'}, use_global_device_ids=true, to_apply=%region_18.19 | all-reduce | flops 3584 | bytes 28672 | tf_op jit(solution)/shard_map/psum | solution.py:257
  (250 shorter events, 356.4 us)
Async XLA Ops:
  7.2 490.4 %copy-start = (f32[512,512]{1,0:T(8,128)S(1)}, f32[512,512]{1,0:T(8,128)}, u32[]{:S(2)}) copy-start(f32[512,512]{1,0:T(8,128)} %param.46) | copy-start | bytes 3145732
  7.2 51.9 %all-gather.8.cloned.1.call-start = ((), (), s32[]{:S(2)}) async-start(), calls=%async_computation.7 | async-start | bytes 3342336 | tf_op jit(solution)/shard_map/all_gather | solution.py:124
  9.1 242.3 %all-gather.10.cloned.1.call-start = ((), (), s32[]{:S(2)}) async-start(), calls=%async_computation.8 | async-start | bytes 10485760 | tf_op jit(solution)/shard_map/all_gather | solution.py:175
  103.2 297.7 %all-gather.18.cloned.1.call-start = ((), (), s32[]{:S(2)}) async-start(), calls=%async_computation.20 | async-start | bytes 10485760 | tf_op jit(solution)/shard_map/all_gather | solution.py:176
  107.3 390.3 %reduce-scatter.16.cloned.1.call-start = ((), (), s32[]{:S(2)}) async-start(), calls=%async_computation.17 | async-start | bytes 2228224 | tf_op jit(solution)/shard_map/reduce_scatter | solution.py:253
  437.7 101.4 %all-gather.12.cloned.1.call-start = ((), (), s32[]{:S(2)}) async-start(), calls=%async_computation.9 | async-start | bytes 1114112 | tf_op jit(solution)/shard_map/all_gather | solution.py:128
  502.0 219.7 %all-gather.14.cloned.1.call-start = ((), (), s32[]{:S(2)}) async-start(), calls=%async_computation.10 | async-start | bytes 4456448 | tf_op jit(solution)/shard_map/all_gather | solution.py:125
  503.8 233.3 %all-gather.16.cloned.1.call-start = ((), (), s32[]{:S(2)}) async-start(), calls=%async_computation.11 | async-start | bytes 4456448 | tf_op jit(solution)/shard_map/all_gather | solution.py:129
  505.7 462.9 %reduce-scatter.10.cloned.1.call-start = ((), (), s32[]{:S(2)}) async-start(), calls=%async_computation.13 | async-start | bytes 20971520 | tf_op jit(solution)/shard_map/reduce_scatter | solution.py:214
  689.1 563.6 %reduce-scatter.12.cloned.1.call-start = ((), (), s32[]{:S(2)}) async-start(), calls=%async_computation.14 | async-start | bytes 20971520 | tf_op jit(solution)/shard_map/reduce_scatter | solution.py:215
  721.6 641.4 %reduce-scatter.18.cloned.1.call-start = ((), (), s32[]{:S(2)}) async-start(), calls=%async_computation.18 | async-start | bytes 8912896 | tf_op jit(solution)/shard_map/reduce_scatter | solution.py:250
  779.1 693.6 %reduce-scatter.20.cloned.1.call-start = ((), (), s32[]{:S(2)}) async-start(), calls=%async_computation.19 | async-start | bytes 8912896 | tf_op jit(solution)/shard_map/reduce_scatter | solution.py:254
  793.9 780.6 %reduce-scatter.8.cloned.1.call-start = ((), (), s32[]{:S(2)}) async-start(), calls=%async_computation.12 | async-start | bytes 12582912 | tf_op jit(solution)/shard_map/reduce_scatter | solution.py:227
  812.5 962.5 %all-reduce.11.cloned.1.call-start = ((), (), s32[]{:S(2)}) async-start(), calls=%async_computation.15 | async-start | bytes 16777216 | tf_op jit(solution)/shard_map/psum | solution.py:236
  848.5 128.4 %copy-start.29 = (f32[256,16]{0,1:T(8,128)S(1)}, f32[256,16]{0,1:T(8,128)}, u32[]{:S(2)}) copy-start(f32[256,16]{0,1:T(8,128)} %copy-done.28) | copy-start | bytes 49156
  848.5 128.4 %copy-start.31 = (f32[256,16]{0,1:T(8,128)S(1)}, f32[256,16]{0,1:T(8,128)}, u32[]{:S(2)}) copy-start(f32[256,16]{0,1:T(8,128)} %copy-done.30) | copy-start | bytes 49156
  1277.8 587.9 %reduce-scatter.14.cloned.1.call-start = ((), (), s32[]{:S(2)}) async-start(), calls=%async_computation.16 | async-start | bytes 6684672 | tf_op jit(solution)/shard_map/reduce_scatter | solution.py:249
  1394.6 103.1 %copy-start.44 = (f32[64,64]{1,0:T(8,128)S(1)}, f32[64,64]{1,0:T(8,128)}, u32[]{:S(2)}) copy-start(f32[64,64]{1,0:T(8,128)} %param.53) | copy-start | bytes 49156
  1394.6 104.3 %copy-start.21 = (f32[64,2048]{1,0:T(8,128)S(1)}, f32[64,2048]{1,0:T(8,128)}, u32[]{:S(2)}) copy-start(f32[64,2048]{1,0:T(8,128)} %param.34) | copy-start | bytes 1572868
  1394.7 106.1 %copy-start.22 = (f32[2048,64]{0,1:T(8,128)S(1)}, f32[2048,64]{0,1:T(8,128)}, u32[]{:S(2)}) copy-start(f32[2048,64]{0,1:T(8,128)} %param.35) | copy-start | bytes 1572868
  1539.4 235.7 %copy-start.27 = (f32[8,256]{1,0:T(8,128)S(1)}, f32[8,256]{1,0:T(8,128)}, u32[]{:S(2)}) copy-start(f32[8,256]{1,0:T(8,128)} %copy-done.26) | copy-start | bytes 24580
  1539.4 235.7 %copy-start.36 = (f32[1,1024]{1,0:T(1,128)S(1)}, f32[1,1024]{1,0:T(1,128)}, u32[]{:S(2)}) copy-start(f32[1,1024]{1,0:T(1,128)} %copy-done.35) | copy-start | bytes 12292
  1580.4 200.3 %copy-start.38 = (f32[8,256]{1,0:T(8,128)S(1)}, f32[8,256]{1,0:T(8,128)}, u32[]{:S(2)}) copy-start(f32[8,256]{1,0:T(8,128)} %copy-done.37) | copy-start | bytes 24580
  1580.4 200.4 %copy-start.33 = (f32[8,256]{1,0:T(8,128)S(1)}, f32[8,256]{1,0:T(8,128)}, u32[]{:S(2)}) copy-start(f32[8,256]{1,0:T(8,128)} %copy-done.32) | copy-start | bytes 24580
  (52 other events, 1551.2 us)
Sparse Core Ops, SparseCore 0:
  10.9 48.1 all-gather.7
  103.3 147.9 all-gather.9
  253.5 147.3 all-gather.17
  437.8 59.7 reduce-scatter.15
  502.1 36.9 all-gather.11
  542.0 49.4 all-gather.13
  594.6 49.2 all-gather.15
  689.2 279.3 reduce-scatter.9
  971.6 281.0 reduce-scatter.11
  1257.7 105.3 reduce-scatter.17
  1368.2 104.3 reduce-scatter.19
  1475.5 98.9 reduce-scatter.7
  1576.9 198.0 all-reduce.10
  1779.4 86.2 reduce-scatter.13
where the time goes:
time: 1910 us; the launch traced here: 1900 us
  waiting for transfers between devices  1120 us (59%)
  matrix products  450 us (24%)
  other arithmetic  167 us (9%)
  local copies, waits for them, and re-layouts  77.6 us (4%)
  blocking collectives  69.2 us (4%)
    reduce_scatter x1, waiting for transfers between devices, body(): lax.psum_scatter(grad_value, 'seq', scatter_dimension=1, tiled=True)  252 us
    psum x1, waiting for transfers between devices, body(): back_normed = lax.psum(input_part, 'mp')  195 us
    all_gather x1, waiting for transfers between devices, body(): lax.all_gather(key_low, 'seq', axis=1, tiled=True)  132 us
    reduce_scatter x1, waiting for transfers between devices, body(): lax.psum_scatter(grad_key, 'seq', scatter_dimension=1, tiled=True)  118 us
    all_gather x1, waiting for transfers between devices, body(): lax.all_gather(value_low, 'seq', axis=1, tiled=True)  96.3 us
    reduce_scatter x1, waiting for transfers between devices, body(): lax.psum_scatter(expand_term, ('dp', 'seq'), scatter_dimension=0, tiled=T...  78.1 us
    reduce_scatter x1, waiting for transfers between devices, body(): lax.psum_scatter(shrink_term, ('dp', 'seq'), scatter_dimension=1, tiled=T...  78 us
    psum x1, blocking collectives, body(): norm_grad, bias_grad = lax.psum((vector_terms, bias_term), ('dp', 'seq'))  63.5 us
  transfers between devices with their start and end apart: 14, of which 12 were waited for; matrix products, arithmetic and copies ran while one was open for 30% of the time, Pallas kernels for 0%

commit v1 on v0

v1 whole, which is shorter than its diff:
```python
import functools
import math

import jax
import jax.numpy as jnp
from jax import lax
from jax.experimental import pallas as pl
from jax.experimental.pallas import tpu as pltpu
from jax.sharding import PartitionSpec as P

HS = 64
ROT = 32
LEN = 1024
BLOCK = 256

highest = lax.Precision.HIGHEST
norm_eps = 1e-05
beta_stats = 0.95
beta_moment = 0.95
rate_matrix = 0.5
rate_vector = 0.03
bf16 = jnp.bfloat16
f32 = jnp.float32
NT = (((1,), (1,)), ((), ()))
TN = (((0,), (0,)), ((), ()))
NN = (((1,), (0,)), ((), ()))


def mm(a, b, dims=NN):
    return lax.dot_general(a, b, dims, preferred_element_type=f32)


def bits_of(size):
    return [1 << i for i in range(size.bit_length() - 1)]


def swap(value, axis, bit):
    size = lax.axis_size(axis)
    return lax.ppermute(value, axis, [(i, i ^ bit) for i in range(size)])


def gather_rows(shard):
    rows, cols = shard.shape
    value = shard[None]
    for axis in ("seq", "dp"):
        inner = value.shape
        lead = 1
        for bit in reversed(bits_of(lax.axis_size(axis))):
            other = swap(value, axis, bit)
            upper = (lax.axis_index(axis) & bit) != 0
            value = jnp.stack([jnp.where(upper, other, value), jnp.where(upper, value, other)], axis=1)
            value = value.reshape((lead * 2,) + inner)
            lead *= 2
        value = value.reshape((1, -1, cols))
    return value.reshape(-1, cols)


def scatter_rows(term, kind=bf16):
    cols = term.shape[1]
    n_dp, n_seq = lax.axis_size("dp"), lax.axis_size("seq")
    value = term.reshape(1, n_dp, -1)
    for axis, size in (("dp", n_dp), ("seq", n_seq)):
        value = value.reshape(size, -1, cols)
        for bit in bits_of(size):
            parts = value.reshape((value.shape[0] // 2, 2) + value.shape[1:])
            index = (lax.axis_index(axis) & bit) // bit
            mine = lax.dynamic_index_in_dim(parts, index, 1, False)
            theirs = lax.dynamic_index_in_dim(parts, 1 - index, 1, False)
            value = mine + swap(theirs.astype(kind), axis, bit).astype(f32)
    return value.reshape(-1, cols)


def sum_all(value, axes):
    for axis in axes:
        for bit in bits_of(lax.axis_size(axis)):
            value = value + swap(value, axis, bit)
    return value


def params(limit=100, **more):
    return pltpu.CompilerParams(vmem_limit_bytes=limit * 2**20 // 2, **more)


def rope_tables():
    lane = jnp.arange(128, dtype=jnp.int32) % HS
    pair = (lane // 2).astype(f32)
    frequency = 10000.0 ** (-2.0 * pair / ROT)
    angles = jnp.arange(LEN, dtype=f32)[:, None] * frequency[None, :]
    turned = (lane < ROT)[None, :]
    cosine = jnp.where(turned, jnp.cos(angles), 1.0)
    sine = jnp.sin(angles)
    to_even = jnp.where(turned & (lane % 2 == 0)[None, :], -sine, 0.0)
    to_odd = jnp.where(turned & (lane % 2 == 1)[None, :], sine, 0.0)
    return cosine, to_even, to_odd


def turn(value, cosine, to_even, to_odd):
    return (
        value * cosine
        + pltpu.roll(value, 127, 1) * to_even
        + pltpu.roll(value, 1, 1) * to_odd
    )


def project_kernel(x_ref, w_ref, c_ref, e_ref, o_ref, out_ref):
    cols = w_ref.shape[1]
    part = cols // 3
    values = mm(x_ref[...], w_ref[...])
    cosine, to_even, to_odd = c_ref[...], e_ref[...], o_ref[...]
    for at in range(0, cols, 128):
        piece = values[:, at : at + 128]
        if at < 2 * part:
            piece = turn(piece, cosine, to_even, to_odd)
        out_ref[:, at : at + 128] = piece.astype(bf16)


def project(rows, weight, tables):
    count, width = rows.shape
    cols = weight.shape[1]
    table = pl.BlockSpec((BLOCK, 128), lambda i: (i, 0))
    return pl.pallas_call(
        project_kernel,
        grid=(count // BLOCK,),
        in_specs=[
            pl.BlockSpec((BLOCK, width), lambda i: (i, 0)),
            pl.BlockSpec((width, cols), lambda i: (0, 0)),
            table,
            table,
            table,
        ],
        out_specs=pl.BlockSpec((BLOCK, cols), lambda i: (i, 0)),
        out_shape=jax.ShapeDtypeStruct((count, cols), bf16),
        compiler_params=params(),
        cost_estimate=pl.CostEstimate(
            flops=2 * count * width * cols, bytes_accessed=2 * (count * (width + cols) + width * cols), transcendentals=0
        ),
        name="project",
    )(rows, weight, *tables)


def attend_kernel(seq_ref, q_ref, k_ref, v_ref, d_ref, c_ref, e_ref, o_ref, ctx_ref, grad_ref, dk_ref, dv_ref):
    part = grad_ref.shape[1] // 3
    pair = pl.program_id(0)
    length, reverse = seq_ref[0], seq_ref[1]
    lane = lax.broadcasted_iota(jnp.int32, (1, 128), 1)
    zero = jnp.zeros((), bf16)
    keys, values = k_ref[...], v_ref[...]
    key_heads, value_heads = [], []
    for head in range(2):
        inside = (lane // HS) == head
        key_heads.append(jnp.where(inside, keys, zero))
        value_heads.append(jnp.where(inside, values, zero))
    dk_ref[...] = jnp.zeros_like(dk_ref)
    dv_ref[...] = jnp.zeros_like(dv_ref)

    low = jnp.where(reverse == 0, 0, LEN - length)
    high = jnp.where(reverse == 0, length, LEN)

    def key_bias(start, size):
        spot = start + lax.broadcasted_iota(jnp.int32, (1, size), 1)
        return jnp.where((spot >= low) & (spot < high), 0.0, -1e30)

    for block in range(LEN // BLOCK):
        begin = block * BLOCK
        stop = begin + BLOCK
        rows = pl.ds(begin, BLOCK)
        query = q_ref[rows, :] * jnp.asarray(1.0 / math.sqrt(HS), bf16)
        back = d_ref[rows, :]
        below = key_bias(0, begin) if begin else None
        q_id = lax.broadcasted_iota(jnp.int32, (BLOCK, BLOCK), 0)
        k_id = lax.broadcasted_iota(jnp.int32, (BLOCK, BLOCK), 1)
        at_diag = jnp.where(k_id < q_id, key_bias(begin, BLOCK), jnp.where(k_id == q_id, 0.0, -1e30))
        context = jnp.zeros((BLOCK, 128), f32)
        grad_query = jnp.zeros((BLOCK, 128), f32)
        for head in range(2):
            inside = (lane // HS) == head
            query_one = jnp.where(inside, query, zero)
            back_one = jnp.where(inside, back, zero)
            scores = mm(query_one, keys[:stop], NT)
            tail = scores[:, begin:] + at_diag
            scores = jnp.concatenate([scores[:, :begin] + below, tail], axis=1) if begin else tail
            top = jnp.max(scores, axis=1, keepdims=True)
            exponent = jnp.exp(scores - top)
            attend = exponent * (1.0 / jnp.sum(exponent, axis=1, keepdims=True))
            attend_low = attend.astype(bf16)
            context += mm(attend_low, value_heads[head][:stop])
            back_attend = mm(back_one, values[:stop], NT)
            delta = jnp.sum(attend * back_attend, axis=1, keepdims=True)
            grad_scores = (attend * (back_attend - delta)).astype(bf16)
            grad_query += mm(grad_scores, key_heads[head][:stop])
            dk_ref[:stop, :] += mm(grad_scores, query_one, TN)
            dv_ref[:stop, :] += mm(attend_low, back_one, TN)
        ctx_ref[rows, :] = context.astype(bf16)
        grad_query = grad_query * (1.0 / math.sqrt(HS))
        grad_query = turn(grad_query, c_ref[rows, :], -e_ref[rows, :], -o_ref[rows, :])
        grad_ref[rows, pl.ds(pl.multiple_of(pair * 128, 128), 128)] = grad_query.astype(bf16)
    grad_key = turn(dk_ref[...], c_ref[...], -e_ref[...], -o_ref[...])
    grad_ref[:, pl.ds(pl.multiple_of(part + pair * 128, 128), 128)] = grad_key.astype(bf16)
    grad_ref[:, pl.ds(pl.multiple_of(2 * part + pair * 128, 128), 128)] = dv_ref[...].astype(bf16)


def attend(info, joint_rows, back_rows, tables):
    cols = joint_rows.shape[1]
    part = cols // 3
    pairs = part // 128
    column = lambda group: pl.BlockSpec((LEN, 128), lambda i, s: (0, group * pairs + i))
    table = pl.BlockSpec((LEN, 128), lambda i, s: (0, 0))
    area = LEN * (LEN + BLOCK) // 2 * (part // HS)
    return pl.pallas_call(
        attend_kernel,
        grid_spec=pltpu.PrefetchScalarGridSpec(
            num_scalar_prefetch=1,
            grid=(pairs,),
            in_specs=[column(0), column(1), column(2), column(0), table, table, table],
            out_specs=[
                pl.BlockSpec((LEN, 128), lambda i, s: (0, i)),
                pl.BlockSpec((LEN, cols), lambda i, s: (0, 0)),
            ],
            scratch_shapes=[pltpu.VMEM((LEN, 128), f32), pltpu.VMEM((LEN, 128), f32)],
        ),
        out_shape=[
            jax.ShapeDtypeStruct((LEN, part), bf16),
            jax.ShapeDtypeStruct((LEN, cols), bf16),
        ],
        compiler_params=params(),
        cost_estimate=pl.CostEstimate(flops=12 * area * 256, bytes_accessed=16 * LEN * part, transcendentals=area),
        name="attend",
    )(info, joint_rows, joint_rows, joint_rows, back_rows, *tables)


def norm_kernel(flip_ref, x_ref, vec_ref, out_ref, own_ref):
    values = x_ref[0].astype(f32)
    centred = values - jnp.mean(values, -1, keepdims=True)
    spread = jnp.mean(centred * centred, -1, keepdims=True)
    normed = centred * lax.rsqrt(spread + norm_eps) * vec_ref[0:1, :] + vec_ref[1:2, :]
    low = normed.astype(bf16)
    out_ref[0] = low

    @pl.when(lax.rem(pl.program_id(0), 2) == flip_ref[0])
    def _():
        own_ref[0] = low


def norm(tokens, vectors, flip):
    seqs, local, width = tokens.shape
    return pl.pallas_call(
        norm_kernel,
        grid_spec=pltpu.PrefetchScalarGridSpec(
            num_scalar_prefetch=1,
            grid=(seqs,),
            in_specs=[
                pl.BlockSpec((1, local, width), lambda i, s: (i, 0, 0)),
                pl.BlockSpec(vectors.shape, lambda i, s: (0, 0)),
            ],
            out_specs=[
                pl.BlockSpec((1, local, width), lambda i, s: (i, 0, 0)),
                pl.BlockSpec((1, local, width), lambda i, s: (i // 2, 0, 0)),
            ],
        ),
        out_shape=[
            jax.ShapeDtypeStruct(tokens.shape, bf16),
            jax.ShapeDtypeStruct((seqs // 2, local, width), bf16),
        ],
        compiler_params=params(),
        cost_estimate=pl.CostEstimate(flops=8 * tokens.size, bytes_accessed=5 * tokens.size, transcendentals=0),
        name="norm",
    )(flip, tokens, vectors)


def norm_back_kernel(order_ref, x_ref, cot_ref, back_ref, vec_ref, *rest):
    out_ref, sums_ref = rest[-2:]
    values = x_ref[0].astype(f32)
    centred = values - jnp.mean(values, -1, keepdims=True)
    spread = jnp.mean(centred * centred, -1, keepdims=True)
    scale = lax.rsqrt(spread + norm_eps)
    xhat = centred * scale
    back = back_ref[0].astype(f32)
    scaled = back * vec_ref[0:1, :]
    shift = jnp.mean(scaled, -1, keepdims=True)
    slope = jnp.mean(scaled * xhat, -1, keepdims=True)
    cot = cot_ref[0].astype(f32)
    out_ref[0] = cot + (scaled - shift - xhat * slope) * scale

    @pl.when(pl.program_id(0) == 0)
    def _():
        sums_ref[...] = jnp.zeros_like(sums_ref)

    sums_ref[0:1, :] += jnp.sum(back * xhat, 0, keepdims=True)
    sums_ref[1:2, :] += jnp.sum(back, 0, keepdims=True)
    sums_ref[2:3, :] += jnp.sum(cot, 0, keepdims=True)


def norm_back(order, tokens, cotangent, back_normed, vectors, earlier=None):
    seqs, local, width = tokens.shape
    count = back_normed.shape[0]
    picked = pl.BlockSpec((1, local, width), lambda i, s: (s[i], 0, 0))
    more = [] if earlier is None else [earlier]
    return pl.pallas_call(
        norm_back_kernel,
        grid_spec=pltpu.PrefetchScalarGridSpec(
            num_scalar_prefetch=1,
            grid=(count,),
            in_specs=[
                picked,
                picked,
                pl.BlockSpec((1, local, width), lambda i, s: (i, 0, 0)),
                pl.BlockSpec(vectors.shape, lambda i, s: (0, 0)),
            ]
            + [pl.BlockSpec(memory_space=pl.ANY)] * len(more),
            out_specs=[picked, pl.BlockSpec((8, width), lambda i, s: (0, 0))],
        ),
        out_shape=[
            jax.ShapeDtypeStruct(tokens.shape, f32),
            jax.ShapeDtypeStruct((8, width), f32),
        ],
        input_output_aliases={5: 0} if more else {},
        compiler_params=params(),
        cost_estimate=pl.CostEstimate(
            flops=30 * back_normed.size, bytes_accessed=10 * back_normed.size, transcendentals=0
        ),
        name="norm_back",
    )(order, tokens, cotangent, back_normed, vectors, *more)


def gelu_tanh(values):
    return jax.nn.gelu(values, approximate=True)


def shampoo(gradient, weight, big, small, big_root, small_root, fan, flipped):
    big_new = beta_stats * big + (1.0 - beta_stats) * lax.dot_general(gradient, gradient, TN, precision=highest)
    small_new = beta_stats * small + (1.0 - beta_stats) * lax.dot_general(gradient, gradient, NT, precision=highest)
    if flipped:
        turned = lax.dot_general(small_root, gradient, TN, precision=highest)
        turned = lax.dot_general(turned, big_root, NT, precision=highest)
    else:
        turned = lax.dot_general(small_root, gradient, NN, precision=highest)
        turned = lax.dot_general(turned, big_root, NN, precision=highest)
    square = jnp.mean(turned * turned)
    weight_new = weight - rate_matrix / math.sqrt(fan) * turned * lax.rsqrt(square + 1e-06)
    return (big_new, small_new, weight_new)


def diagonal_rule(values, moment, gradient):
    moment_new = beta_moment * moment + (1.0 - beta_moment) * gradient * gradient
    return (moment_new, values - rate_vector * gradient / (jnp.sqrt(moment_new) + 1e-08))


def body(
    tokens,
    cotangent,
    lengths,
    orientation,
    joint_weight,
    output_weight,
    expand_weight,
    shrink_weight,
    norm_params,
    expand_bias,
    norm_moment,
    bias_moment,
    joint_left,
    joint_right,
    joint_left_root,
    joint_right_root,
    output_left,
    output_right,
    output_left_root,
    output_right_root,
    expand_left,
    expand_right,
    expand_left_root,
    expand_right_root,
    shrink_left,
    shrink_right,
    shrink_left_root,
    shrink_right_root,
):
    n_mp, n_seq = lax.axis_size("mp"), lax.axis_size("seq")
    mp_index, seq_index = lax.axis_index("mp"), lax.axis_index("seq")
    seqs, local, width = tokens.shape
    rows = seqs * local
    share = norm_params.shape[1]
    per = seqs // n_seq
    paired = n_mp == 2 and per == 2
    flip = mp_index if paired else jnp.zeros((), jnp.int32)
    flip_one = jnp.reshape(flip, (1,)).astype(jnp.int32)

    output_t, shrink_t = output_weight.T, shrink_weight.T
    if paired:
        other_vectors = swap(norm_params, "mp", 1)
        upper = mp_index != 0
        vectors = jnp.concatenate(
            [jnp.where(upper, other_vectors, norm_params), jnp.where(upper, norm_params, other_vectors)], axis=1
        )
    else:
        vectors = lax.all_gather(norm_params, "mp", axis=1, tiled=True)
    joint_full = gather_rows(joint_weight.astype(bf16))
    output_full = gather_rows(output_t.astype(bf16))
    expand_full = gather_rows(expand_weight.astype(bf16))
    shrink_full = gather_rows(shrink_t.astype(bf16))

    def own_share(values):
        return lax.dynamic_slice_in_dim(values, mp_index * share, share, values.ndim - 1)

    def to_whole(values):
        return lax.all_to_all(values, "seq", 0, 0, tiled=True)

    tables = rope_tables()
    normed, normed_own = norm(tokens, vectors, flip_one)
    normed_rows = normed.reshape(rows, width)
    cot_rows = cotangent.reshape(rows, width)
    ids = [flip, 1 - flip] if paired else list(range(per))

    if paired:
        first = to_whole(normed_own).reshape(LEN, width)
        normed_seqs = [first, swap(first, "mp", 1)]
    else:
        split = normed.reshape(n_seq, per, local, width)
        normed_seqs = [to_whole(split[:, t]).reshape(LEN, width) for t in range(per)]
    back_context = mm(cot_rows, output_full).astype(bf16).reshape(n_seq, per, local, -1)
    part = back_context.shape[-1]

    contexts, grads = [], []
    for t, which in enumerate(ids):
        back_one = lax.dynamic_index_in_dim(back_context, which, 1, False)
        back_one = to_whole(back_one).reshape(LEN, part)
        spot = seq_index * per + which
        info = jnp.stack(
            [lax.dynamic_index_in_dim(lengths, spot, 0, False), lax.dynamic_index_in_dim(orientation, spot, 0, False)]
        )
        joint_rows = project(normed_seqs[t], joint_full, tables)
        context_one, grad_one = attend(info, joint_rows, back_one, tables)
        contexts.append(to_whole(context_one.reshape(n_seq, local, part)))
        grads.append(grad_one)

    pre_act = mm(normed_rows, expand_full) + expand_bias
    active, gelu_back = jax.vjp(gelu_tanh, pre_act)
    active_low = active.astype(bf16)
    grad_pre = gelu_back(mm(cot_rows, shrink_full))[0].astype(bf16)
    bias_term = jnp.sum(grad_pre.astype(f32), 0)
    back_ffn = mm(grad_pre, expand_full, NT).astype(bf16).reshape(n_seq, per, local, width)

    if paired:
        first_even = flip == 0
        context = jnp.stack(
            [jnp.where(first_even, contexts[0], contexts[1]), jnp.where(first_even, contexts[1], contexts[0])], axis=1
        )
    else:
        context = jnp.stack(contexts, axis=1)
    context = context.reshape(rows, part)
    branch = mm(context, output_full, NT) + mm(active_low, shrink_full, NT)
    branch = branch.reshape(seqs, local, width)
    if paired:
        away = lax.dynamic_slice_in_dim(branch, (1 - mp_index) * share, share, 2)
        summed = own_share(branch) + swap(away.astype(bf16), "mp", 1).astype(f32)
    else:
        summed = lax.psum_scatter(branch, "mp", scatter_dimension=2, tiled=True)
    block_output = (own_share(tokens).astype(f32) + summed + norm_params[2]).astype(bf16)

    back_seqs = [mm(grad_one, joint_full, NT) for grad_one in grads]
    cot_sum = None
    if paired:
        back_own = back_seqs[0] + swap(back_seqs[1].astype(bf16), "mp", 1).astype(f32)
        back_own = to_whole(back_own.astype(bf16).reshape(n_seq, local, width))
        ffn_own = lax.dynamic_index_in_dim(back_ffn, flip, 1, False)
        ffn_away = lax.dynamic_index_in_dim(back_ffn, 1 - flip, 1, False)
        total = (ffn_own.astype(f32) + swap(ffn_away, "mp", 1).astype(f32) + back_own.astype(f32)).astype(bf16)
        total_other = swap(total, "mp", 1)
        order = jnp.arange(n_seq, dtype=jnp.int32) * 2
        partial_grad, sums = norm_back(order + flip, tokens, cotangent, total, vectors)
        input_grad, sums_other = norm_back(order + 1 - flip, tokens, cotangent, total_other, vectors, partial_grad)
        sums = sums + sums_other
    else:
        pieces = [lax.psum(one, "mp") for one in back_seqs]
        pieces = [to_whole(one.astype(bf16).reshape(n_seq, local, width)) for one in pieces]
        total = jnp.stack(pieces, axis=1).astype(f32) + lax.psum(back_ffn.astype(f32), "mp")
        total = total.astype(bf16).reshape(seqs, local, width)
        input_grad, sums = norm_back(jnp.arange(seqs, dtype=jnp.int32), tokens, cotangent, total, vectors)

    joint_term = mm(normed_seqs[0], grads[0], TN)
    for one, grad_one in zip(normed_seqs[1:], grads[1:]):
        joint_term = joint_term + mm(one, grad_one, TN)
    expand_term = mm(normed_rows, grad_pre, TN)
    output_term = mm(cot_rows, context, TN)
    shrink_term = mm(cot_rows, active_low, TN)
    expand_grad = scatter_rows(expand_term)
    shrink_grad = scatter_rows(shrink_term)
    joint_grad = scatter_rows(joint_term)
    output_grad = scatter_rows(output_term)
    norm_grad = sum_all(own_share(sums[:3]), ("dp", "seq"))
    bias_grad = sum_all(bias_term, ("dp", "seq"))

    fans = (width, width // 32, width, 4 * width)
    joint_right_new, joint_left_new, joint_new = shampoo(
        joint_grad, joint_weight, joint_right, joint_left, joint_right_root, joint_left_root, fans[0], False
    )
    output_left_new, output_right_new, output_new = shampoo(
        output_grad, output_t, output_left, output_right, output_left_root, output_right_root, fans[1], True
    )
    expand_right_new, expand_left_new, expand_new = shampoo(
        expand_grad, expand_weight, expand_right, expand_left, expand_right_root, expand_left_root, fans[2], False
    )
    shrink_left_new, shrink_right_new, shrink_new = shampoo(
        shrink_grad, shrink_t, shrink_left, shrink_right, shrink_left_root, shrink_right_root, fans[3], True
    )
    norm_moment_new, norm_params_new = diagonal_rule(norm_params, norm_moment, norm_grad)
    bias_moment_new, bias_new = diagonal_rule(expand_bias, bias_moment, bias_grad)
    return (
        block_output,
        input_grad,
        joint_grad,
        output_grad.T,
        expand_grad,
        shrink_grad.T,
        norm_grad,
        bias_grad,
        joint_left_new,
        joint_right_new,
        output_left_new,
        output_right_new,
        expand_left_new,
        expand_right_new,
        shrink_left_new,
        shrink_right_new,
        joint_new,
        output_new.T,
        expand_new,
        shrink_new.T,
        norm_moment_new,
        bias_moment_new,
        norm_params_new,
        bias_new,
    )


def solution(mesh):
    data = P("dp", "seq", None)
    rows = P(("dp", "seq"), "mp")
    cols = P("mp", ("dp", "seq"))
    vector = P(None, "mp")
    placed = (data, data, P("dp"), P("dp"), rows, cols, rows, cols, vector, P("mp"), vector, P("mp")) + (rows,) * 16
    out_placed = (
        (P("dp", "seq", "mp"), data, rows, cols, rows, cols, vector, P("mp"))
        + (rows,) * 8
        + (rows, cols, rows, cols, vector, P("mp"), vector, P("mp"))
    )
    return jax.shard_map(body, mesh=mesh, in_specs=placed, out_specs=out_placed, check_vma=False)
```

time: 1910 us -> 833 us (0.44)
  waiting for transfers between devices: 1120 us -> 242 us
  matrix products: 450 us -> 234 us
  Pallas kernels: 0 us -> 109 us
  other arithmetic: 167 us -> 68.5 us
  starting transfers between devices: 0.79 us -> 79.5 us
  blocking collectives: 69.2 us -> 0 us
    reduce_scatter x7 -> x0, waiting for transfers between devices: 625 us -> none  [the longest x1 252 us: body(): lax.psum_scatter(grad_value, 'seq', scatter_dimension=1, tiled=True)]
    all_gather x6 -> x0, waiting for transfers between devices: 296 us -> none  [the longest x1 132 us: body(): lax.all_gather(key_low, 'seq', axis=1, tiled=True)]
    dot_general x34 -> x29, matrix products: 450 us -> 234 us  [the longest x13 127 us: mm(): return lax.dot_general(a, b, dims, preferred_element_type=f32)]
    ppermute x0 -> x46, waiting for transfers between devices: none -> 216 us  [swap(): return lax.ppermute(value, axis, [(i, i ^ bit) for i in range(size)])]
    psum x1 -> x0, waiting for transfers between devices: 195 us -> none  [body(): back_normed = lax.psum(input_part, 'mp')]
    pallas_call x0 -> x7, Pallas kernels: none -> 109 us  [the longest x2 72.9 us: attend(): pl.pallas_call(attend_kernel, grid_spec=pltpu.PrefetchScalarGridSpec(num_...]
    convert_element_type x8 -> x3, other arithmetic: 79.2 us -> 13.3 us  [the longest x1 5.14 us: body(): (own_share(tokens).astype(f32) + summed + norm_params[2]).astype(bf16)]
    psum x1 -> x0, blocking collectives: 63.5 us -> none  [body(): norm_grad, bias_grad = lax.psum((vector_terms, bias_term), ('dp', 'seq'))]
  transfers between devices with their start and end apart: 14 -> 52, of which waited for: 12 -> 20; matrix products, arithmetic and copies ran while one was open for 30% -> 44% of each run, Pallas kernels for 0% -> 12%
where the time goes in v1:
time: 833 us; the launch traced here: 822 us
  waiting for transfers between devices  242 us (29%)
  matrix products  234 us (28%)
  Pallas kernels  109 us (13%)
  local copies, waits for them, and re-layouts  83.7 us (10%)
  starting transfers between devices  79.5 us (10%)
  other arithmetic  68.5 us (8%)
    ppermute x46, waiting for transfers between devices, swap(): return lax.ppermute(value, axis, [(i, i ^ bit) for i in range(size)])  216 us
    dot_general x13, matrix products, mm(): return lax.dot_general(a, b, dims, preferred_element_type=f32)  127 us
    pallas_call x2, Pallas kernels, attend(): pl.pallas_call(attend_kernel, grid_spec=pltpu.PrefetchScalarGridSpec(num_...  72.9 us
    dot_general x4, matrix products, shampoo(): lax.dot_general(gradient, gradient, TN, precision=highest)  55 us
    ppermute x46, starting transfers between devices, swap(): return lax.ppermute(value, axis, [(i, i ^ bit) for i in range(size)])  47.8 us
    all_to_all x6, starting transfers between devices, to_whole(): return lax.all_to_all(values, 'seq', 0, 0, tiled=True)  31.7 us
    all_to_all x6, waiting for transfers between devices, to_whole(): return lax.all_to_all(values, 'seq', 0, 0, tiled=True)  25.9 us
    unnamed x153, local copies, waits for them, and re-layouts  25 us
  transfers between devices with their start and end apart: 52, of which 20 were waited for; matrix products, arithmetic and copies ran while one was open for 44% of the time, Pallas kernels for 12%

profile of v1, /device:TPU:0, one launch (start us, length us, event | category | flops | bytes accessed | tf_op | source)
XLA Modules:
  0.0 822.0 jit_solution(16324038479622914607)
XLA Ops:
  63.6 28.1 %collective-permute-done.2 = bf16[2,1,64,1536]{3,2,0,1:T(8,128)(2,1)S(1)} collective-permute-done((bf16[2,1,64,1536]{3,2,0,1:T(8,128)(2,1)S(1)}, bf16[2,1,64,1536]{3,2,0,1:T(8,128)(2,1)S(1)}, u32[]{:S(2)}, u32[]{:S(2)}) %collective-permute-start.2) | collective-permute-done | bytes 393248 | tf_op jit(solution)/shard_map/ppermute | solution.py:39
  93.3 10.4 %collective-permute-done.11 = bf16[2,1,64,2048]{3,2,0,1:T(8,128)(2,1)S(1)} collective-permute-done((bf16[2,1,64,2048]{3,2,0,1:T(8,128)(2,1)S(1)}, bf16[2,1,64,2048]{3,2,0,1:T(8,128)(2,1)S(1)}, u32[]{:S(2)}, u32[]{:S(2)}) %collective-permute-start.11) | collective-permute-done | bytes 524320 | tf_op jit(solution)/shard_map/ppermute | solution.py:39
  165.4 11.4 %all-to-all-done.1 = bf16[4,256,512]{2,1,0:T(8,128)(2,1)} async-done(((bf16[4,256,512]{2,1,0:T(8,128)(2,1)}), bf16[4,256,512]{2,1,0:T(8,128)(2,1)}, u32[]{:S(2)}, u32[]{:S(2)}) %all-to-all-start.1) | async-done | bytes 1048608 | tf_op jit(solution)/shard_map/all_to_all | solution.py:406
  184.2 36.5 %attend.2 = (bf16[1024,512]{1,0:T(8,128)(2,1)S(1)}, bf16[1024,1536]{1,0:T(8,128)(2,1)}) custom-call(s32[2]{0:T(128)S(1)} %pad_add_fusion.seq_ref, bf16[1024,1536]{1,0:T(8,128)(2,1)} %project.2.q_ref.k_ref.v_ref, bf16[1024,1536]{1,0:T(8,128)(2,1)} %project.2.q_ref.k_ref.v_ref, bf16[1024,1536]{1,0:T(8,128)(2,1)} %project.2.q_ref.k_ref.v_ref, ...), custom_call_target="tpu_custom_call" | custom-call | flops 16106127360 | bytes 8388608 | tf_op jit(solution)/shard_map/attend/pallas_call | solution.py:209
  236.4 21.7 %multiply_convert_fusion = (bf16[2048,2048]{1,0:T(8,128)(2,1)}, f32[2048,2048]{1,0:T(8,128)}) fusion(f32[2048]{0:T(1024)S(1)} %copy-done.68, bf16[2048,1024]{1,0:T(8,128)(2,1)} %bitcast.368, bf16[1024,2048]{1,0:T(8,128)(2,1)S(1)} %bitcast.365), kind=kOutput, calls=%fused_computation.17 | convolution fusion | flops 8631877632 | bytes 33562624 | tf_op jit(solution)/shard_map/dot_general | solution.py:30
  258.0 11.6 %fusion.51 = f32[2048,1024]{0,1:T(8,128)S(1)} fusion(bf16[2048,2048]{1,0:T(8,128)(2,1)} %get-tuple-element.97, bf16[2048,1024]{1,0:T(8,128)(2,1)S(1)} %bitcast.344), kind=kOutput, calls=%fused_computation.199 | convolution fusion | flops 8589934592 | bytes 20971520 | tf_op jit(solution)/shard_map/dot_general | solution.py:30
  290.3 36.4 %attend.3 = (bf16[1024,512]{1,0:T(8,128)(2,1)}, bf16[1024,1536]{1,0:T(8,128)(2,1)}) custom-call(s32[2]{0:T(128)S(1)} %pad_add_fusion.1.seq_ref, bf16[1024,1536]{1,0:T(8,128)(2,1)} %project.3.q_ref.k_ref.v_ref, bf16[1024,1536]{1,0:T(8,128)(2,1)} %project.3.q_ref.k_ref.v_ref, bf16[1024,1536]{1,0:T(8,128)(2,1)} %project.3.q_ref.k_ref.v_ref, ...), custom_call_target="tpu_custom_call" | custom-call | flops 16106127360 | bytes 8388608 | tf_op jit(solution)/shard_map/attend/pallas_call | solution.py:209
  358.8 14.5 %all-to-all-done.4 = bf16[4,256,512]{2,1,0:T(8,128)(2,1)S(1)} async-done(((bf16[4,256,512]{2,1,0:T(8,128)(2,1)}), bf16[4,256,512]{2,1,0:T(8,128)(2,1)S(1)}, u32[]{:S(2)}, u32[]{:S(2)}) %all-to-all-start.4) | async-done | bytes 1048608 | tf_op jit(solution)/shard_map/all_to_all | solution.py:406
  407.7 15.9 %collective-permute-done.36 = bf16[2,64,2048]{2,1,0:T(8,128)(2,1)} collective-permute-done((bf16[2,64,2048]{2,1,0:T(8,128)(2,1)}, bf16[2,64,2048]{2,1,0:T(8,128)(2,1)}, u32[]{:S(2)}, u32[]{:S(2)}) %collective-permute-start.36) | collective-permute-done | bytes 524320 | tf_op jit(solution)/shard_map/ppermute | solution.py:39
  426.9 24.8 %collective-permute-done.28 = bf16[2,64,512]{2,1,0:T(8,128)(2,1)S(1)} collective-permute-done((bf16[2,64,512]{2,1,0:T(8,128)(2,1)S(1)}, bf16[2,64,512]{2,1,0:T(8,128)(2,1)S(1)}, u32[]{:S(2)}, u32[]{:S(2)}) %collective-permute-start.28) | collective-permute-done | bytes 131104 | tf_op jit(solution)/shard_map/ppermute | solution.py:39
  455.2 13.8 %collective-permute-done.29 = bf16[1,64,512]{2,1,0:T(8,128)(2,1)S(1)} collective-permute-done((bf16[1,64,512]{2,1,0:T(8,128)(2,1)S(1)}, bf16[1,64,512]{2,1,0:T(8,128)(2,1)S(1)}, u32[]{:S(2)}, u32[]{:S(2)}) %collective-permute-start.29) | collective-permute-done | bytes 65568 | tf_op jit(solution)/shard_map/ppermute | solution.py:39
  476.0 19.0 %multiply_reduce_fusion = (f32[]{:T(128)}, f32[64,2048]{1,0:T(8,128)S(1)}) fusion(f32[2048,64]{1,0:T(8,128)S(1)} %fusion.28, f32[2048,2048]{1,0:T(8,128)} %param.54), kind=kOutput, calls=%fused_computation.103 | convolution fusion | flops 3221487616 | bytes 17825796 | tf_op jit(solution)/shard_map/dot_general | solution.py:334
  511.3 19.6 %multiply_add_fusion = f32[2048,2048]{1,0:T(8,128)} fusion(f32[2048,2048]{1,0:T(8,128)} %param.52, bf16[1,64,2048]{2,1,0:T(8,128)(2,1)S(1)} %collective-permute-done.37, f32[2,64,2048]{2,1,0:T(8,128)S(1)} %bitcast_add_fusion.3, s32[]{:T(128)S(6)} %select_n.506), kind=kOutput, calls=%fused_computation.14 | convolution fusion | flops 3234070528 | bytes 34340868 | tf_op jit(solution)/shard_map/dot_general | solution.py:330
  538.7 17.7 %collective-permute-done.16 = bf16[1,256,2048]{2,1,0:T(8,128)(2,1)S(1)} collective-permute-done((bf16[1,256,2048]{2,1,0:T(8,128)(2,1)S(1)}, bf16[1,256,2048]{2,1,0:T(8,128)(2,1)S(1)}, u32[]{:S(2)}, u32[]{:S(2)}) %collective-permute-start.16) | collective-permute-done | bytes 1048608 | tf_op jit(solution)/shard_map/ppermute | solution.py:39
  567.6 12.4 %fusion.10 = f32[1536,1536]{1,0:T(8,128)} fusion(f32[64,1536]{1,0:T(8,128)S(1)} %add_bitcast_fusion.1, f32[1536,1536]{1,0:T(8,128)} %param.41), kind=kOutput, calls=%fused_computation.19 | convolution fusion | flops 1819017216 | bytes 19267584 | tf_op jit(solution)/shard_map/dot_general | solution.py:330
  582.6 11.6 %fusion.48 = f32[2048,1024]{1,0:T(8,128)S(1)} fusion(bf16[2048,2048]{1,0:T(8,128)(2,1)} %get-tuple-element.97, bf16[1024,2048]{1,0:T(8,128)(2,1)S(1)} %bitcast.369), kind=kOutput, calls=%fused_computation.196 | convolution fusion | flops 8589934592 | bytes 20971520 | tf_op jit(solution)/shard_map/dot_general | solution.py:30
  594.2 24.3 %convert_reduce_fusion = (f32[2048]{0:T(1024)S(1)}, bf16[2048,2048]{1,0:T(8,128)(2,1)}) fusion(f32[2048,2048]{1,0:T(8,128)} %get-tuple-element.98, f32[2048]{0:T(1024)S(1)} %copy-done.68, bf16[2048,1024]{1,0:T(8,128)(2,1)S(1)} %bitcast.346, bf16[1024,2048]{1,0:T(8,128)(2,1)S(1)} %bitcast.370), kind=kOutput, calls=%fused_computation.16 | convolution fusion | flops 8686401536 | bytes 33570816 | tf_op jit(solution)/shard_map/dot_general | solution.py:30
  618.5 11.4 %fusion.11 = f32[2,2,256,2048]{3,2,1,0:T(8,128)S(1)} fusion(bf16[2,2,256,2048]{3,2,1,0:T(8,128)(2,1)S(1)} %bitcast.364, bf16[2048,2048]{1,0:T(8,128)(2,1)} %get-tuple-element.102), kind=kOutput, calls=%fused_computation.20 | convolution fusion | flops 8589934592 | bytes 20971520 | tf_op jit(solution)/shard_map/dot_general | solution.py:30
  635.5 11.3 %convolution_convert_fusion = bf16[2048,1024]{1,0:T(8,128)(2,1)S(1)} fusion(bf16[2048,2048]{1,0:T(8,128)(2,1)} %get-tuple-element.102, bf16[1024,2048]{1,0:T(8,128)(2,1)S(1)} %bitcast.366), kind=kOutput, calls=%fused_computation.36 | convolution fusion | flops 8592031744 | bytes 16777216 | tf_op jit(solution)/shard_map/dot_general | solution.py:30
  660.8 18.1 %collective-permute-done.43 = f32[2048]{0:T(1024)S(1)} collective-permute-done((f32[2048]{0:T(1024)S(1)}, f32[2048]{0:T(1024)S(1)}, u32[]{:S(2)}, u32[]{:S(2)}) %collective-permute-start.43) | collective-permute-done | bytes 8224 | tf_op jit(solution)/shard_map/ppermute | solution.py:39
  714.5 27.8 %collective-permute-done.18 = bf16[8,256,512]{2,1,0:T(8,128)(2,1)} collective-permute-done((bf16[8,256,512]{2,1,0:T(8,128)(2,1)}, bf16[8,256,512]{2,1,0:T(8,128)(2,1)}, u32[]{:S(2)}, u32[]{:S(2)}) %collective-permute-start.18) | collective-permute-done | bytes 2097184 | tf_op jit(solution)/shard_map/ppermute | solution.py:39
  747.4 19.7 %multiply_add_fusion.1 = f32[2048,2048]{1,0:T(8,128)} fusion(f32[2048,2048]{1,0:T(8,128)} %param.49, f32[64,2048]{1,0:T(8,128)S(1)} %add_bitcast_fusion), kind=kOutput, calls=%fused_computation.15 | convolution fusion | flops 3233808384 | bytes 34078720 | tf_op jit(solution)/shard_map/dot_general | solution.py:330
  767.1 19.6 %collective-permute-done.21.back_ref = bf16[4,256,1024]{2,1,0:T(8,128)(2,1)S(1)} collective-permute-done((bf16[4,256,1024]{2,1,0:T(8,128)(2,1)S(1)}, bf16[4,256,1024]{2,1,0:T(8,128)(2,1)S(1)}, u32[]{:S(2)}, u32[]{:S(2)}) %collective-permute-start.21) | collective-permute-done | bytes 2097184 | tf_op jit(solution)/shard_map/ppermute | solution.py:39
  797.2 15.0 %multiply_reduce_fusion.1 = (f32[]{:T(128)}, f32[64,2048]{1,0:T(8,128)S(1)}) fusion(f32[2048,64]{1,0:T(8,128)S(1)} %fusion.53, f32[2048,2048]{1,0:T(8,128)} %param.51), kind=kOutput, calls=%fused_computation.105 | convolution fusion | flops 3221487616 | bytes 17825796 | tf_op jit(solution)/shard_map/dot_general | solution.py:337
  (383 shorter events, 364.5 us)
Async XLA Ops:
  5.5 54.9 %collective-permute-start.10 = (bf16[1,64,2048]{2,1,0:T(8,128)(2,1)}, bf16[1,64,2048]{2,1,0:T(8,128)(2,1)}, u32[]{:S(2)}, u32[]{:S(2)}) collective-permute-start(bf16[1,64,2048]{2,1,0:T(8,128)(2,1)} %convert_bitcast_fusion.2), channel_id=1, source_target_pairs={{0,2},{1,3},{2,0},{3,1},{4,6},{5,7},{6,4},{7,5},{8,10},{9,11},{10,... | collective-permute-start | bytes 786440 | tf_op jit(solution)/shard_map/ppermute | solution.py:39
  9.8 47.5 %collective-permute-start.1 = (bf16[1,64,1536]{2,1,0:T(8,128)(2,1)}, bf16[1,64,1536]{2,1,0:T(8,128)(2,1)}, u32[]{:S(2)}, u32[]{:S(2)}) collective-permute-start(bf16[1,64,1536]{2,1,0:T(8,128)(2,1)} %convert_bitcast_fusion.3), channel_id=1, source_target_pairs={{0,2},{1,3},{2,0},{3,1},{4,6},{5,7},{6,4},{7,5},{8,10},{9,11},{10,... | collective-permute-start | bytes 589832 | tf_op jit(solution)/shard_map/ppermute | solution.py:39
  43.5 98.7 %all-to-all-start = ((bf16[4,256,1024]{2,1,0:T(8,128)(2,1)}), bf16[4,256,1024]{2,1,0:T(8,128)(2,1)S(1)}, u32[]{:S(2)}, u32[]{:S(2)}) async-start(bf16[4,256,1024]{2,1,0:T(8,128)(2,1)} %copy-done.2), calls=%async_computation | async-start | bytes 4194304 | tf_op jit(solution)/shard_map/all_to_all | solution.py:406
  58.2 33.4 %collective-permute-start.2 = (bf16[2,1,64,1536]{3,2,0,1:T(8,128)(2,1)S(1)}, bf16[2,1,64,1536]{3,2,0,1:T(8,128)(2,1)S(1)}, u32[]{:S(2)}, u32[]{:S(2)}) collective-permute-start(bf16[2,1,64,1536]{3,2,0,1:T(8,128)(2,1)S(1)} %maximum_bitcast_fusion.6), channel_id=1, source_target_pairs={{0,1},{1,0},{2,3},{3,2},{4,5},{5,4},{6,7},{7,6},{8,9},{9,8},{10,11... | collective-permute-start | bytes 1179656 | tf_op jit(solution)/shard_map/ppermute | solution.py:39
  61.6 42.2 %collective-permute-start.11 = (bf16[2,1,64,2048]{3,2,0,1:T(8,128)(2,1)S(1)}, bf16[2,1,64,2048]{3,2,0,1:T(8,128)(2,1)S(1)}, u32[]{:S(2)}, u32[]{:S(2)}) collective-permute-start(bf16[2,1,64,2048]{3,2,0,1:T(8,128)(2,1)S(1)} %maximum_bitcast_fusion.4), channel_id=1, source_target_pairs={{0,1},{1,0},{2,3},{3,2},{4,5},{5,4},{6,7},{7,6},{8,9},{9,8},{10,11... | collective-permute-start | bytes 1572872 | tf_op jit(solution)/shard_map/ppermute | solution.py:39
  63.5 42.9 %collective-permute-start.8 = (bf16[2,1,256,512]{3,2,0,1:T(8,128)(2,1)S(1)}, bf16[2,1,256,512]{3,2,0,1:T(8,128)(2,1)S(1)}, u32[]{:S(2)}, u32[]{:S(2)}) collective-permute-start(bf16[2,1,256,512]{3,2,0,1:T(8,128)(2,1)S(1)} %maximum_bitcast_fusion.3), channel_id=1, source_target_pairs={{0,4},{4,0},{8,12},{12,8},{1,5},{5,1},{9,13},{13,9},{2,6},{6,2},{1... | collective-permute-start | bytes 1572872 | tf_op jit(solution)/shard_map/ppermute | solution.py:39
  104.9 44.8 %collective-permute-start.12 = (bf16[1,256,2048]{2,1,0:T(8,128)(2,1)}, bf16[1,256,2048]{2,1,0:T(8,128)(2,1)}, u32[]{:S(2)}, u32[]{:S(2)}) collective-permute-start(bf16[1,256,2048]{2,1,0:T(8,128)(2,1)} %bitcast.52), channel_id=1, source_target_pairs={{0,8},{4,12},{8,0},{12,4},{1,9},{5,13},{9,1},{13,5},{2,10},{6,14},... | collective-permute-start | bytes 3145736 | tf_op jit(solution)/shard_map/ppermute | solution.py:39
  113.9 40.4 %collective-permute-start.4 = (bf16[2,1,256,1536]{3,2,0,1:T(8,128)(2,1)}, bf16[2,1,256,1536]{3,2,0,1:T(8,128)(2,1)}, u32[]{:S(2)}, u32[]{:S(2)}) collective-permute-start(bf16[2,1,256,1536]{3,2,0,1:T(8,128)(2,1)} %maximum_bitcast_fusion.2), channel_id=1, source_target_pairs={{0,4},{4,0},{8,12},{12,8},{1,5},{5,1},{9,13},{13,9},{2,6},{6,2},{1... | collective-permute-start | bytes 4718600 | tf_op jit(solution)/shard_map/ppermute | solution.py:39
  142.2 34.6 %all-to-all-start.1 = ((bf16[4,256,512]{2,1,0:T(8,128)(2,1)}), bf16[4,256,512]{2,1,0:T(8,128)(2,1)}, u32[]{:S(2)}, u32[]{:S(2)}) async-start(bf16[4,256,512]{2,1,0:T(8,128)(2,1)} %bitcast.362), calls=%async_computation.1 | async-start | bytes 2097152 | tf_op jit(solution)/shard_map/all_to_all | solution.py:406
  154.0 79.4 %collective-permute-start.13 = (bf16[2,1,256,2048]{3,2,0,1:T(8,128)(2,1)}, bf16[2,1,256,2048]{3,2,0,1:T(8,128)(2,1)}, u32[]{:S(2)}, u32[]{:S(2)}) collective-permute-start(bf16[2,1,256,2048]{3,2,0,1:T(8,128)(2,1)} %maximum_bitcast_fusion), channel_id=1, source_target_pairs={{0,4},{4,0},{8,12},{12,8},{1,5},{5,1},{9,13},{13,9},{2,6},{6,2},{1... | collective-permute-start | bytes 6291464 | tf_op jit(solution)/shard_map/ppermute | solution.py:39
  158.1 116.6 %collective-permute-start.9 = (bf16[1024,1024]{1,0:T(8,128)(2,1)S(1)}, bf16[1024,1024]{1,0:T(8,128)(2,1)}, u32[]{:S(2)}, u32[]{:S(2)}) collective-permute-start(bf16[1024,1024]{1,0:T(8,128)(2,1)S(1)} %bitcast.337), channel_id=1, source_target_pairs={{0,16},{16,0},{1,17},{17,1},{2,18},{18,2},{3,19},{19,3},{4,20},{20... | collective-permute-start | bytes 6291464 | tf_op jit(solution)/shard_map/ppermute | solution.py:39
  176.8 105.1 %all-to-all-start.3 = ((bf16[4,256,512]{2,1,0:T(8,128)(2,1)}), bf16[4,256,512]{2,1,0:T(8,128)(2,1)}, u32[]{:S(2)}, u32[]{:S(2)}) async-start(bf16[4,256,512]{2,1,0:T(8,128)(2,1)} %bitcast.361), calls=%async_computation.3 | async-start | bytes 2097152 | tf_op jit(solution)/shard_map/all_to_all | solution.py:406
  274.6 72.6 %collective-permute-start.34 = (bf16[2,256,2048]{2,1,0:T(8,128)(2,1)}, bf16[2,256,2048]{2,1,0:T(8,128)(2,1)}, u32[]{:S(2)}, u32[]{:S(2)}) collective-permute-start(bf16[2,256,2048]{2,1,0:T(8,128)(2,1)} %fusion.17), channel_id=1, source_target_pairs={{0,4},{4,0},{8,12},{12,8},{1,5},{5,1},{9,13},{13,9},{2,6},{6,2},{1... | collective-permute-start | bytes 6291464 | tf_op jit(solution)/shard_map/ppermute | solution.py:39
  281.9 60.0 %all-to-all-start.2 = ((bf16[4,256,512]{2,1,0:T(8,128)(2,1)}), bf16[4,256,512]{2,1,0:T(8,128)(2,1)S(1)}, u32[]{:S(2)}, u32[]{:S(2)}) async-start(bf16[4,256,512]{2,1,0:T(8,128)(2,1)} %bitcast.340), calls=%async_computation.2 | async-start | bytes 2097152 | tf_op jit(solution)/shard_map/all_to_all | solution.py:406
  341.4 56.0 %collective-permute-start.20 = (bf16[1024,1024]{1,0:T(8,128)(2,1)}, bf16[1024,1024]{1,0:T(8,128)(2,1)}, u32[]{:S(2)}, u32[]{:S(2)}) collective-permute-start(bf16[1024,1024]{1,0:T(8,128)(2,1)} %convolution_convert_fusion.2), channel_id=1, source_target_pairs={{0,16},{16,0},{1,17},{17,1},{2,18},{18,2},{3,19},{19,3},{4,20},{20... | collective-permute-start | bytes 6291464 | tf_op jit(solution)/shard_map/ppermute | solution.py:39
  352.0 40.8 %collective-permute-start.35 = (bf16[1,256,2048]{2,1,0:T(8,128)(2,1)}, bf16[1,256,2048]{2,1,0:T(8,128)(2,1)}, u32[]{:S(2)}, u32[]{:S(2)}) collective-permute-start(bf16[1,256,2048]{2,1,0:T(8,128)(2,1)} %dynamic-slice_convert_fusion.2), channel_id=1, source_target_pairs={{0,8},{4,12},{8,0},{12,4},{1,9},{5,13},{9,1},{13,5},{2,10},{6,14},... | collective-permute-start | bytes 3145736 | tf_op jit(solution)/shard_map/ppermute | solution.py:39
  358.3 67.2 %collective-permute-start.23 = (bf16[1,256,1536]{2,1,0:T(8,128)(2,1)}, bf16[1,256,1536]{2,1,0:T(8,128)(2,1)}, u32[]{:S(2)}, u32[]{:S(2)}) collective-permute-start(bf16[1,256,1536]{2,1,0:T(8,128)(2,1)} %dynamic-slice_convert_fusion.4), channel_id=1, source_target_pairs={{0,8},{4,12},{8,0},{12,4},{1,9},{5,13},{9,1},{13,5},{2,10},{6,14},... | collective-permute-start | bytes 2359304 | tf_op jit(solution)/shard_map/ppermute | solution.py:39
  401.1 286.8 %all-to-all-start.5 = ((bf16[4,256,1024]{2,1,0:T(8,128)(2,1)}), bf16[4,256,1024]{2,1,0:T(8,128)(2,1)}, u32[]{:S(2)}, u32[]{:S(2)}) async-start(bf16[4,256,1024]{2,1,0:T(8,128)(2,1)} %bitcast.80), calls=%async_computation.5 | async-start | bytes 4194304 | tf_op jit(solution)/shard_map/all_to_all | solution.py:406
  425.2 49.0 %collective-permute-start.37 = (bf16[1,64,2048]{2,1,0:T(8,128)(2,1)S(1)}, bf16[1,64,2048]{2,1,0:T(8,128)(2,1)S(1)}, u32[]{:S(2)}, u32[]{:S(2)}) collective-permute-start(bf16[1,64,2048]{2,1,0:T(8,128)(2,1)S(1)} %dynamic-slice_convert_fusion.7), channel_id=1, source_target_pairs={{0,2},{1,3},{2,0},{3,1},{4,6},{5,7},{6,4},{7,5},{8,10},{9,11},{10,... | collective-permute-start | bytes 786440 | tf_op jit(solution)/shard_map/ppermute | solution.py:39
  455.1 79.6 %collective-permute-start.24 = (bf16[2,64,1536]{2,1,0:T(8,128)(2,1)}, bf16[2,64,1536]{2,1,0:T(8,128)(2,1)}, u32[]{:S(2)}, u32[]{:S(2)}) collective-permute-start(bf16[2,64,1536]{2,1,0:T(8,128)(2,1)} %fusion.32), channel_id=1, source_target_pairs={{0,1},{1,0},{2,3},{3,2},{4,5},{5,4},{6,7},{7,6},{8,9},{9,8},{10,11... | collective-permute-start | bytes 1179656 | tf_op jit(solution)/shard_map/ppermute | solution.py:39
  648.5 48.7 %collective-permute-start.19 = (bf16[4,256,1024]{2,1,0:T(8,128)(2,1)}, bf16[4,256,1024]{2,1,0:T(8,128)(2,1)}, u32[]{:S(2)}, u32[]{:S(2)}) collective-permute-start(bf16[4,256,1024]{2,1,0:T(8,128)(2,1)} %dynamic-slice_bitcast_fusion), channel_id=1, source_target_pairs={{0,16},{16,0},{1,17},{17,1},{2,18},{18,2},{3,19},{19,3},{4,20},{20... | collective-permute-start | bytes 6291464 | tf_op jit(solution)/shard_map/ppermute | solution.py:39
  660.1 82.1 %collective-permute-start.18 = (bf16[8,256,512]{2,1,0:T(8,128)(2,1)}, bf16[8,256,512]{2,1,0:T(8,128)(2,1)}, u32[]{:S(2)}, u32[]{:S(2)}) collective-permute-start(bf16[8,256,512]{2,1,0:T(8,128)(2,1)} %dynamic-slice_convert_fusion.1), channel_id=1, source_target_pairs={{0,16},{16,0},{1,17},{17,1},{2,18},{18,2},{3,19},{19,3},{4,20},{20... | collective-permute-start | bytes 6291464 | tf_op jit(solution)/shard_map/ppermute | solution.py:39
  701.6 85.0 %collective-permute-start.21 = (bf16[4,256,1024]{2,1,0:T(8,128)(2,1)S(1)}, bf16[4,256,1024]{2,1,0:T(8,128)(2,1)S(1)}, u32[]{:S(2)}, u32[]{:S(2)}) collective-permute-start(bf16[4,256,1024]{2,1,0:T(8,128)(2,1)S(1)} %fusion.14.back_ref), channel_id=1, source_target_pairs={{0,16},{16,0},{1,17},{17,1},{2,18},{18,2},{3,19},{19,3},{4,20},{20... | collective-permute-start | bytes 6291464 | tf_op jit(solution)/shard_map/ppermute | solution.py:39
  712.0 35.4 %collective-permute-start.33 = (bf16[1,64,2048]{2,1,0:T(8,128)(2,1)S(1)}, bf16[1,64,2048]{2,1,0:T(8,128)(2,1)S(1)}, u32[]{:S(2)}, u32[]{:S(2)}) collective-permute-start(bf16[1,64,2048]{2,1,0:T(8,128)(2,1)S(1)} %dynamic-slice_convert_fusion.8), channel_id=1, source_target_pairs={{0,2},{1,3},{2,0},{3,1},{4,6},{5,7},{6,4},{7,5},{8,10},{9,11},{10,... | collective-permute-start | bytes 786440 | tf_op jit(solution)/shard_map/ppermute | solution.py:39
  (104 other events, 2134.2 us)
